TPU v7x, 512 devices: a whole 4x4x16 slice. The times are simulated.
512 devices in a mesh: curve: 128 (over y, z, core), rep: 4 (over x).
Axes of the slice: x: 4, y: 4, z: 16, core: 2. Of those that a mesh axis runs over, the one named last changes fastest.
Arguments:
- offsets: float32 [65536, 3, 256], P(('curve', 'rep')), may hold values from -1 to 1
- masses: float32 [65536, 256], P(('curve', 'rep')), may hold values from 0.1 to 2
- destination: int32 [65536, 1], P(('curve', 'rep')), may hold values from 0 to 127; in each aligned block of 128 rows (0 to 127, 128 to 255, ...) at most 2 rows name the same one
- leaf_ids: int32 [65536], P(('curve', 'rep')), may hold values from 0 to 1023
Outputs:
- owned_offsets: float32 [131072, 3, 256], P(('curve', 'rep'))
- owned_masses: float32 [131072, 256], P(('curve', 'rep'))
- leaf_moments: float32 [35, 524288], P(None, ('curve', 'rep'))
- top_tree: float32 [35, 9344], replicated
Inputs may be any that keep to these rules, and one draw needn't show every extreme that they name: `destination`: among the blocks of one device at most 2 name the same curve index, and in every draw some curve index is named by exactly 2 blocks of some device.
All inputs are finite; a program needn't handle non-finite values.
Results may differ from a plain program's by a relative error of at most 0.0001.
Values sent between devices are 32-bit elements; how exact they have to be, the bound alone decides.
A program may use at most 64 MiB of HBM per device.

v0:
```python
import math

import jax
import jax.numpy as jnp
import numpy as np
from jax import lax
from jax.sharding import PartitionSpec as P

LEAVES_DEV = 1024


def moment_terms():
    listed = []
    for degree in range(5):
        for a in range(degree, -1, -1):
            for c in range(degree - a, -1, -1):
                listed.append((a, c, degree - a - c))
    return listed


def yz_pairs():
    return [(c, e) for c in range(5) for e in range(5 - c)]


def term_selection():
    pairs = yz_pairs()
    return np.array([a * 15 + pairs.index((c, e)) for a, c, e in moment_terms()], dtype=np.int32)


def octant_table():
    listed = moment_terms()
    table = np.zeros((8, 35, 35), dtype=np.float32)
    for octant in range(8):
        signs = (2 * (octant % 2) - 1, 2 * (octant // 2 % 2) - 1, 2 * (octant // 4) - 1)
        for row, upper in enumerate(listed):
            for column, lower in enumerate(listed):
                if all((lower[i] <= upper[i] for i in range(3))):
                    value = 0.125 * 2.0 ** (-sum(upper))
                    for i in range(3):
                        value = (
                            value
                            * math.comb(upper[i], lower[i])
                            * signs[i] ** (upper[i] - lower[i])
                        )
                    table[octant, row, column] = value
    return table


def lift_level(children):
    count = children.shape[1]
    shift_table = jnp.asarray(octant_table())
    grouped = children.reshape(children.shape[0], count // 8, 8)
    return jnp.einsum("oab,bno->an", shift_table, grouped, precision=lax.Precision.HIGHEST)


def block_moments(places, weights):
    count = places.shape[0]
    points = places.shape[2]
    group_size = 64 if count % 64 == 0 else count
    selection = term_selection()

    def block_group(parcel):
        spots, loads = parcel
        xcoord = spots[:, 0, :]
        ycoord = spots[:, 1, :]
        zcoord = spots[:, 2, :]
        xpowers = [loads]
        ypowers = [jnp.ones_like(ycoord)]
        zpowers = [jnp.ones_like(zcoord)]
        for level in range(4):
            xpowers.append(xpowers[-1] * xcoord)
            ypowers.append(ypowers[-1] * ycoord)
            zpowers.append(zpowers[-1] * zcoord)
        xstack = jnp.stack(xpowers)
        yzstack = jnp.stack([ypowers[c] * zpowers[e] for c, e in yz_pairs()])
        products = jnp.einsum("agp,kgp->gak", xstack, yzstack, precision=lax.Precision.HIGHEST) * (
            1.0 / points
        )
        return jnp.take(products.reshape(products.shape[0], 75), selection, axis=1)

    spots = places.reshape(count // group_size, group_size, 3, points)
    loads = weights.reshape(count // group_size, group_size, points)
    result = lax.map(block_group, (spots, loads))
    return result.reshape(count, 35)


def shards(offsets, masses, destination, leaf_ids):
    peers = lax.axis_size("curve")
    reps = lax.axis_size("rep")
    points = offsets.shape[2]
    per_peer = 2 * offsets.shape[0] // peers
    total = peers * per_peer
    target = destination[:, 0]
    onehot = (target[:, None] == jnp.arange(peers, dtype=jnp.int32)[None, :]).astype(jnp.int32)
    before = jnp.cumsum(onehot, axis=0) - onehot
    within = jnp.sum(before * onehot, axis=1)
    slot_index = target * per_peer + within
    send_places = (
        jnp.zeros((total, 3, points), jnp.float32)
        .at[slot_index]
        .set(offsets)
        .reshape(peers, per_peer, 3, points)
    )
    send_masses = (
        jnp.zeros((total, points), jnp.float32)
        .at[slot_index]
        .set(masses)
        .reshape(peers, per_peer, points)
    )
    send_leaves = (
        jnp.full((total,), -1, jnp.int32).at[slot_index].set(leaf_ids).reshape(peers, per_peer)
    )
    places = lax.all_to_all(send_places, "curve", split_axis=0, concat_axis=0, tiled=True)
    weights = lax.all_to_all(send_masses, "curve", split_axis=0, concat_axis=0, tiled=True)
    leaves = lax.all_to_all(send_leaves, "curve", split_axis=0, concat_axis=0, tiled=True)
    count = places.shape[0] * places.shape[1]
    moments = block_moments(places.reshape(count, 3, points), weights.reshape(count, points))
    got_moments = moments.reshape(places.shape[0], places.shape[1], 35)
    owned_offsets = places.reshape(total, 3, points)
    owned_masses = weights.reshape(total, points)
    flat_moments = got_moments.reshape(total, 35)
    flat_leaves = leaves.reshape(total)
    leaf_count = LEAVES_DEV
    leaf_hot = (flat_leaves[:, None] == jnp.arange(leaf_count, dtype=jnp.int32)[None, :]).astype(
        jnp.float32
    )
    leaf_moments = lax.dot_general(
        flat_moments, leaf_hot, (((0,), (0,)), ((), ())), precision=lax.Precision.HIGHEST
    )
    level_one = lift_level(leaf_moments)
    level_two = lift_level(level_one)
    whole_two = lax.all_gather(level_two, ("curve", "rep"), axis=1, tiled=True)
    own_two = level_two.shape[1]
    placed = lax.dynamic_update_slice(
        jnp.zeros((35, reps * own_two), jnp.float32),
        level_two,
        (jnp.int32(0), lax.axis_index("rep") * own_two),
    )
    partial_three = lift_level(placed)
    group_three = lax.psum(partial_three, "rep")
    level_three = lax.all_gather(group_three, "curve", axis=1, tiled=True)
    count_three = level_three.shape[1]
    root_count = (count_three + 7) // 8
    padded = jnp.pad(level_three, ((0, 0), (0, root_count * 8 - count_three)))
    level_four = lift_level(padded)
    top_tree = jnp.concatenate([whole_two, level_three, level_four], axis=1)
    return (owned_offsets, owned_masses, leaf_moments, top_tree)


def solution(mesh):
    placed = (
        P(("curve", "rep"), None, None),
        P(("curve", "rep"), None),
        P(("curve", "rep"), None),
        P(("curve", "rep")),
    )
    return jax.shard_map(
        shards,
        mesh=mesh,
        in_specs=placed,
        out_specs=(
            P(("curve", "rep"), None, None),
            P(("curve", "rep"), None),
            P(None, ("curve", "rep")),
            P(),
        ),
        check_vma=False,
    )
```

profile of v0, /device:TPU:1, one launch (start us, length us, event | category | flops | bytes accessed | tf_op | source)
XLA Modules:
  0.0 344.6 jit_solution(1544834220750241869)
XLA Ops:
  7.2 0.8 fusion.22
  8.0 0.2 reduce_window_sum.11
  8.1 0.8 select_reduce_fusion
  9.0 0.7 fusion.24
  9.6 1.1 scatter_custom_fusion.2
  10.8 0.8 all_to_all.14
  11.5 20.6 %all-to-all-start.2 = ((s32[128,1,2]{2,1,0:T(1,128)}), s32[128,1,2]{2,1,0:T(1,128)S(1)}, u32[]{:S(2)}, u32[]{:S(2)}) async-start(s32[128,1,2]{2,1,0:T(1,128)} %bitcast.4), calls=%async_computation.2 | async-start | bytes 131072 | tf_op jit(solution)/shard_map/all_to_all | solution.py:115
  32.1 1.4 scatter_custom_fusion.1
  33.5 0.8 reshape.263
  34.4 12.7 %all-to-all-done.2 = s32[128,1,2]{2,1,0:T(1,128)S(1)} async-done(((s32[128,1,2]{2,1,0:T(1,128)}), s32[128,1,2]{2,1,0:T(1,128)S(1)}, u32[]{:S(2)}, u32[]{:S(2)}) %all-to-all-start.2) | async-done | bytes 1056 | tf_op jit(solution)/shard_map/all_to_all | solution.py:115
  47.1 6.6 %all-to-all-start.1 = ((f32[128,2,256]{2,1,0:T(2,128)}), f32[128,2,256]{2,1,0:T(2,128)S(1)}, u32[]{:S(2)}, u32[]{:S(2)}) async-start(f32[128,2,256]{2,1,0:T(2,128)} %reshape.263), calls=%async_computation.1 | async-start | bytes 524288 | tf_op jit(solution)/shard_map/all_to_all | solution.py:114
  53.6 0.3 copy.67
  53.9 0.1 broadcast_in_dim.32
  54.1 4.4 %scatter_fusion = f32[256,3,256]{2,1,0:T(4,128)S(1)} fusion(f32[256,3,256]{2,1,0:T(4,128)S(1)} %broadcast_in_dim.32, s32[128]{0:T(128)S(1)} %fusion.24, f32[128,3,256]{2,1,0:T(4,128)S(1)} %copy.67), kind=kCustom, calls=%fused_computation.1 | custom fusion | bytes 1180160 | tf_op jit(solution)/shard_map/scatter | solution.py:101
  58.4 1.3 copy.68
  59.7 16.5 %all-to-all-done.1 = f32[128,2,256]{2,1,0:T(2,128)S(1)} async-done(((f32[128,2,256]{2,1,0:T(2,128)}), f32[128,2,256]{2,1,0:T(2,128)S(1)}, u32[]{:S(2)}, u32[]{:S(2)}) %all-to-all-start.1) | async-done | bytes 262176 | tf_op jit(solution)/shard_map/all_to_all | solution.py:114
  76.2 7.3 %all-to-all-start = ((f32[128,2,3,256]{3,1,2,0:T(2,128)}), f32[128,2,3,256]{3,1,2,0:T(2,128)S(1)}, u32[]{:S(2)}, u32[]{:S(2)}) async-start(f32[128,2,3,256]{3,1,2,0:T(2,128)} %copy.68), calls=%async_computation | async-start | bytes 1572864 | tf_op jit(solution)/shard_map/all_to_all | solution.py:113
  83.6 0.2 all-gather.2.cloned.1.call-start
  83.8 0.5 broadcast.93
  84.3 0.8 reduce.3
  85.1 0.1 eq.34
  85.3 0.2 reshape_reshape.6
  85.5 41.7 %all-to-all-done = f32[128,2,3,256]{3,1,2,0:T(2,128)S(1)} async-done(((f32[128,2,3,256]{3,1,2,0:T(2,128)}), f32[128,2,3,256]{3,1,2,0:T(2,128)S(1)}, u32[]{:S(2)}, u32[]{:S(2)}) %all-to-all-start) | async-done | bytes 786464 | tf_op jit(solution)/shard_map/all_to_all | solution.py:113
  127.2 0.3 copy.69
  127.4 0.5 reshape_reshape.7
  128.0 12.1 %while.11 = (s32[]{:T(128)}, f32[4,64,35]{1,0,2:T(4,128)S(1)}, f32[4,64,256]{2,1,0:T(8,128)S(1)}, f32[4,64,3,256]{3,1,0,2:T(8,128)S(1)}, s32[]{:T(128)}, /*index=5*/s32[35]{0:T(128)S(1)}, s32[]{:T(128)}) while((s32[]{:T(128)}, f32[4,64,35]{1,0,2:T(4,128)S(1)}, f32[4,64,256]{2,1,0:T(8,128)S(1)}, ...), condition=%wide.region_5.6_spmd.clone, body=%wide.region_4.5_spmd.sunk.clone.sunk | while | flops 15275713 | bytes 5134977 | solution.py:83
  128.4 1.7 convolution_multiply_fusion.2
  130.3 0.6 gather_fusion
  131.4 1.7 convolution_multiply_fusion.2
  133.4 0.6 gather_fusion
  134.5 1.7 convolution_multiply_fusion.2
  136.4 0.6 gather_fusion
  137.5 1.7 convolution_multiply_fusion.2
  139.4 0.6 gather_fusion
  140.3 0.5 fusion.15
  140.8 0.2 copy.74
  141.0 0.6 convolution_bitcast_fusion
  141.6 0.9 constant_dynamic-update-slice_fusion.4
  142.5 0.9 reshape.264
  143.4 1.4 reshape.262
  144.8 0.2 convolution_bitcast_fusion.3
  145.0 8.5 %psum.7 = f32[35,8]{0,1:T(8,128)S(1)} all-reduce(f32[35,8]{0,1:T(8,128)S(1)} %convolution_bitcast_fusion.3), channel_id=1, replica_groups=mesh['curve'=128,'rep'=4] {'rep'}, use_global_device_ids=true, to_apply=%region_7.8 | all-reduce | flops 280 | bytes 2240 | tf_op jit(solution)/shard_map/psum | solution.py:140
  153.5 85.0 %all_gather.7 = f32[35,1024]{0,1:T(8,128)S(1)} all-gather(f32[35,8]{0,1:T(8,128)S(1)} %psum.7), channel_id=1, replica_groups=mesh['curve'=128,'rep'=4] {'curve'}, dimensions={1}, use_global_device_ids=true | all-gather | bytes 144480 | tf_op jit(solution)/shard_map/all_gather | solution.py:141
  238.5 0.2 copy.81
  238.7 0.7 convolution_bitcast_fusion.1
  239.3 94.3 %all-gather.2.cloned.1.call-done = f32[35,8192]{0,1:T(8,128)} async-done(((f32[35,16]{0,1:T(8,128)}), f32[35,8192]{0,1:T(8,128)}) %all-gather.2.cloned.1.call-update) | async-done | bytes 1146896 | tf_op jit(solution)/shard_map/all_gather | solution.py:132
  333.7 2.9 copy.80
  336.6 1.2 pad_maximum_fusion
  (100 shorter events, 2.3 us)
Async XLA Ops:
  7.2 46.5 %copy-start.1 = (f32[128,3,256]{2,0,1:T(8,128)S(1)}, f32[128,3,256]{2,0,1:T(8,128)}, u32[]{:S(2)}) copy-start(f32[128,3,256]{2,0,1:T(8,128)} %param.11) | copy-start | bytes 1179652
  11.5 35.5 %all-to-all-start.2 = ((s32[128,1,2]{2,1,0:T(1,128)}), s32[128,1,2]{2,1,0:T(1,128)S(1)}, u32[]{:S(2)}, u32[]{:S(2)}) async-start(s32[128,1,2]{2,1,0:T(1,128)} %bitcast.4), calls=%async_computation.2 | async-start | bytes 131072 | tf_op jit(solution)/shard_map/all_to_all | solution.py:115
  47.1 29.2 %all-to-all-start.1 = ((f32[128,2,256]{2,1,0:T(2,128)}), f32[128,2,256]{2,1,0:T(2,128)S(1)}, u32[]{:S(2)}, u32[]{:S(2)}) async-start(f32[128,2,256]{2,1,0:T(2,128)} %reshape.263), calls=%async_computation.1 | async-start | bytes 524288 | tf_op jit(solution)/shard_map/all_to_all | solution.py:114
  76.2 50.9 %all-to-all-start = ((f32[128,2,3,256]{3,1,2,0:T(2,128)}), f32[128,2,3,256]{3,1,2,0:T(2,128)S(1)}, u32[]{:S(2)}, u32[]{:S(2)}) async-start(f32[128,2,3,256]{3,1,2,0:T(2,128)} %copy.68), calls=%async_computation | async-start | bytes 1572864 | tf_op jit(solution)/shard_map/all_to_all | solution.py:113
  83.6 250.1 %all-gather.2.cloned.1.call-start = ((), (), s32[]{:S(2)}) async-start(), calls=%async_computation.3 | async-start | bytes 4202496 | tf_op jit(solution)/shard_map/all_gather | solution.py:132
  85.5 42.5 %copy-start.3 = (s32[35]{0:T(128)S(1)}, s32[35]{0:T(128)}, u32[]{:S(2)}) copy-start(s32[35]{0:T(128)} %constant.186) | copy-start | bytes 424
  128.0 13.0 %copy-start = (f32[8,35,35]{2,1,0:T(8,128)S(1)}, f32[8,35,35]{2,1,0:T(8,128)}, u32[]{:S(2)}) copy-start(f32[8,35,35]{2,1,0:T(8,128)} %constant.61.clone) | copy-start | bytes 117604
  140.8 4.0 %copy-start.2 = (f32[35,1024]{1,0:T(8,128)}, f32[35,1024]{1,0:T(8,128)S(1)}, u32[]{:S(2)}) copy-start(f32[35,1024]{1,0:T(8,128)S(1)} %fusion.15) | copy-start | bytes 430084
Sparse Core Ops, SparseCore 0:
  142.6 190.9 all-gather.1
where the time goes:
time: 345 us
  waiting for transfers between devices  165 us (48%)
  blocking collectives  93.4 us (27%)
  starting transfers between devices  34.6 us (10%)
  local copies, waits for them, and re-layouts  21.3 us (6%)
  between operations  14.3 us (4%)
  matrix products  9.74 us (3%)
  other arithmetic  5.25 us (2%)
    all_gather x1, waiting for transfers between devices, shards(): whole_two = lax.all_gather(level_two, ('curve', 'rep'), axis=1, tiled=True)  94.3 us
    all_gather x1, blocking collectives, shards(): level_three = lax.all_gather(group_three, 'curve', axis=1, tiled=True)  85 us
    all_to_all x1, waiting for transfers between devices, shards(): lax.all_to_all(send_places, 'curve', split_axis=0, concat_axis=0, tiled=T...  41.7 us
    all_to_all x1, starting transfers between devices, shards(): lax.all_to_all(send_leaves, 'curve', split_axis=0, concat_axis=0, tiled=T...  20.6 us
    all_to_all x1, waiting for transfers between devices, shards(): lax.all_to_all(send_masses, 'curve', split_axis=0, concat_axis=0, tiled=T...  16.5 us
    all_to_all x1, waiting for transfers between devices, shards(): lax.all_to_all(send_leaves, 'curve', split_axis=0, concat_axis=0, tiled=T...  12.7 us
    psum x1, blocking collectives, shards(): group_three = lax.psum(partial_three, 'rep')  8.49 us
    all_to_all x1, starting transfers between devices, shards(): lax.all_to_all(send_places, 'curve', split_axis=0, concat_axis=0, tiled=T...  7.3 us
  transfers between devices with their start and end apart: 4, of which 4 were waited for; matrix products, arithmetic and copies ran while one was open for 4% of the time, Pallas kernels for 0%

commit v1 on v0

v1 whole, which is shorter than its diff:
```python
import functools
import math

import jax
import jax.numpy as jnp
import numpy as np
from jax import lax
from jax.experimental import pallas as pl
from jax.experimental.pallas import tpu as pltpu
from jax.sharding import PartitionSpec as P

MESH = pl.DeviceIdType.MESH
NY, NZ, NX = 4, 16, 4
PEERS = 128
LEAVES_DEV = 1024
TERMS = 35
ROWS = 40
TILE_ROWS = 6
FIRST = 16


def moment_terms():
    listed = []
    for degree in range(5):
        for a in range(degree, -1, -1):
            for c in range(degree - a, -1, -1):
                listed.append((a, c, degree - a - c))
    return listed


def octant_table():
    listed = moment_terms()
    table = np.zeros((8, ROWS, ROWS), dtype=np.float32)
    for octant in range(8):
        signs = (2 * (octant % 2) - 1, 2 * (octant // 2 % 2) - 1, 2 * (octant // 4) - 1)
        for row, upper in enumerate(listed):
            for column, lower in enumerate(listed):
                if all(lower[i] <= upper[i] for i in range(3)):
                    value = 0.125 * 2.0 ** (-sum(upper))
                    for i in range(3):
                        value = (
                            value
                            * math.comb(upper[i], lower[i])
                            * signs[i] ** (upper[i] - lower[i])
                        )
                    table[octant, row, column] = value
    return table.reshape(8 * ROWS, ROWS)


def fold_table():
    table = np.zeros((64, TERMS * 8), dtype=np.float32)
    for term in range(TERMS):
        table[term, term * 8 : term * 8 + 8] = 1.0 / 256.0
    return table


def split3(value):
    high = value.astype(jnp.bfloat16)
    rest = value - high.astype(jnp.float32)
    middle = rest.astype(jnp.bfloat16)
    low = (rest - middle.astype(jnp.float32)).astype(jnp.bfloat16)
    return high, middle, low


NN = (((1,), (0,)), ((), ()))
NT = (((1,), (1,)), ((), ()))


def dot(a, b, dims):
    return lax.dot_general(a, b, dims, preferred_element_type=jnp.float32)


def dot_right(exact, value, dims=NN):
    high, middle, low = split3(value)
    return dot(exact, high, dims) + (dot(exact, middle, dims) + dot(exact, low, dims))


def dot_left(value, exact, dims=NN):
    high, middle, low = split3(value)
    return dot(high, exact, dims) + (dot(middle, exact, dims) + dot(low, exact, dims))


def iota(shape, axis):
    return lax.broadcasted_iota(jnp.int32, shape, axis)


def ones_where(mask):
    return jnp.where(mask, 1.0, 0.0).astype(jnp.bfloat16)


def raise_by(table, value, octant):
    moved = dot_right(table, value)
    total = jnp.zeros_like(value)
    for g in range(8):
        total = total + jnp.where(octant == g, moved[g * ROWS : (g + 1) * ROWS], 0.0)
    return total


def particle_moments(planes, fold):
    x, y, z, m = [jnp.transpose(plane) for plane in planes]
    sums = [None] * TERMS
    listed = moment_terms()
    for part in range(32):
        rows = slice(part * 8, part * 8 + 8)
        coordinates = (x[rows], y[rows], z[rows])
        made = {}
        for index, term in enumerate(listed):
            if sum(term) == 0:
                made[term] = m[rows]
            else:
                axis = [i for i in range(3) if term[i] > 0][0]
                below = tuple(term[i] - (1 if i == axis else 0) for i in range(3))
                made[term] = made[below] * coordinates[axis]
            sums[index] = made[term] if part == 0 else sums[index] + made[term]
    return dot_right(fold, jnp.concatenate(sums, axis=0))


def turn_blocks(value):
    sub = iota((8, 128), 0)
    group = iota((8, 128), 1) // 16
    for bit in (1, 2, 4):
        up = pltpu.roll(pltpu.roll(value, bit, 0), 128 - 16 * bit, 1)
        down = up if bit == 4 else pltpu.roll(pltpu.roll(value, 8 - bit, 0), 16 * bit, 1)
        moved = jnp.where((sub & bit) != 0, up, down)
        value = jnp.where(((sub ^ group) & bit) == 0, value, moved)
    return value


def exchange(
    offsets_hbm,
    masses_hbm,
    target_hbm,
    leaves_hbm,
    table_hbm,
    fold_hbm,
    landed,
    leaf_hbm,
    tree_hbm,
    offsets,
    masses,
    target,
    leaves,
    table_ref,
    fold_ref,
    bulk_size,
    slip_size,
    load_sems,
    packed,
    slips,
    got_slips,
    leaf_moments,
    tree,
    tiles,
    z_size,
    ready,
    leaf_sem,
    tree_sem,
    slip_out,
    slip_in,
    bulk_out,
    bulk_in,
    z_out,
    z_in,
    gather_out,
    gather_in,
    core_out,
    core_in,
):
    me = lax.axis_index("curve")
    x = lax.axis_index("rep")
    y, z, c = me // 32, (me // 2) % NZ, me % 2
    rank8 = c * NX + x

    def place(py, pz, pc):
        return (py * NZ + pz) * 2 + pc

    loads = [
        pltpu.make_async_copy(source, kept, load_sems.at[index])
        for index, (source, kept) in enumerate(
            (
                (target_hbm, target),
                (leaves_hbm, leaves),
                (masses_hbm, masses),
                (offsets_hbm, offsets),
                (fold_hbm, fold_ref),
                (table_hbm, table_ref),
            )
        )
    ]
    for load in loads:
        load.start()

    barrier = pltpu.get_barrier_semaphore()
    near = [(dy, dc) for dy in range(NY) for dc in range(2) if dy or dc]
    for dz in range(1, NZ):
        pl.semaphore_signal(
            barrier,
            inc=1,
            device_id={"curve": place(y, (z + dz) % NZ, c)},
            device_id_type=MESH,
        )
    for dy, dc in near:
        pl.semaphore_signal(
            barrier,
            inc=1,
            device_id={"curve": place((y + dy) % NY, z, (c + dc) % 2)},
            device_id_type=MESH,
        )
    group = [(dx, dc) for dx in range(NX) for dc in range(2) if dx or dc]
    for dx, dc in group:
        if dx:
            pl.semaphore_signal(
                barrier,
                inc=1,
                device_id={"curve": place(y, z, (c + dc) % 2), "rep": (x + dx) % NX},
                device_id_type=MESH,
            )

    for load in loads:
        load.wait()

    table = table_ref[...].astype(jnp.bfloat16)
    aim = target[...]
    leaf = leaves[...]
    named = ones_where(iota((PEERS, 128), 0) == aim)
    earlier = ones_where(iota((128, 128), 0) < iota((128, 128), 1))
    before = dot(named, earlier, NN)
    within = jnp.sum(before * named.astype(jnp.float32), axis=0, keepdims=True)
    slot = 2 * aim + within.astype(jnp.int32)

    planes = [offsets[0], offsets[1], offsets[2], masses[...]]
    moments = particle_moments(planes, fold_ref[...].astype(jnp.bfloat16))
    moments = jnp.where(iota((64, 128), 0) == TERMS, leaf.astype(jnp.float32), moments)
    nothing = jnp.zeros_like(moments)
    halves = jnp.concatenate(
        [
            jnp.concatenate([moments, nothing], axis=1),
            jnp.concatenate([nothing, moments], axis=1),
        ],
        axis=0,
    )
    twice = 2 * iota((128, 128), 0)
    picks = jnp.concatenate([ones_where(slot == twice), ones_where(slot == twice + 1)], axis=1)
    slips[...] = dot_right(picks, halves, NT)

    pl.semaphore_wait(barrier, 28)
    for dy, dc in near:
        pl.semaphore_signal(
            ready,
            inc=1,
            device_id={"curve": place((y + dy) % NY, z, (c + dc) % 2)},
            device_id_type=MESH,
        )

    spread = ones_where(iota((256, 128), 0) == slot)
    for index, plane in enumerate(planes):
        packed[index] = dot_right(spread, plane)

    pl.semaphore_wait(ready, 7)

    def peer(step):
        turn, inner = step // 8, 7 - step % 8
        dz = NZ // 2 + (1 - turn % 2) * (turn // 2) - (turn % 2) * ((turn + 1) // 2)
        return place((y + inner // 2) % NY, (z + dz) % NZ, (c + inner % 2) % 2)

    def send_slip(step, carry):
        to = peer(step)
        pltpu.make_async_remote_copy(
            slips.at[pl.ds(to, 1)],
            got_slips.at[pl.ds(me, 1)],
            slip_out,
            slip_in,
            device_id={"curve": to},
            device_id_type=MESH,
        ).start()
        return carry

    lax.fori_loop(0, PEERS - 1, send_slip, 0)
    pltpu.make_async_copy(
        slips.at[pl.ds(me, 1)], got_slips.at[pl.ds(me, 1)], slip_in
    ).start()

    def send_block(step, carry):
        to = peer(step)
        pltpu.make_async_remote_copy(
            packed.at[:, pl.ds(2 * to, 2)],
            landed.at[:, pl.ds(2 * me, 2)],
            bulk_out,
            bulk_in,
            device_id={"curve": to},
            device_id_type=MESH,
        ).start()
        return carry

    lax.fori_loop(0, FIRST, send_block, 0)
    pltpu.make_async_copy(
        packed.at[:, pl.ds(2 * me, 2)], landed.at[:, pl.ds(2 * me, 2)], bulk_in
    ).start()

    pltpu.make_async_copy(got_slips, got_slips, slip_in).wait()
    turned = jnp.transpose(got_slips[...])
    held = jnp.concatenate([turned[:ROWS], turned[64 : 64 + ROWS]], axis=1)
    cell = held[TERMS : TERMS + 1].astype(jnp.int32)
    one = raise_by(table, held, cell & 7)
    two = raise_by(table, one, (cell >> 3) & 7)
    three = raise_by(table, two, (cell >> 6) & 7)
    level_two = dot_left(two, ones_where(iota((128, 256), 0) % 16 == cell >> 6), NT)
    pair = dot_right(
        ones_where(iota((8, 256), 0) == cell >> 9),
        jnp.concatenate([three, jnp.zeros((64 - ROWS, 256), jnp.float32)], axis=0),
        NT,
    )
    own_lanes = iota((8, 128), 1) // 16 == iota((8, 128), 0)
    for row in range(5):
        tiles[y, z // 8, z % 8, row, pl.ds(rank8, 1)] = jnp.sum(
            jnp.where(own_lanes, level_two[8 * row : 8 * row + 8], 0.0),
            axis=0,
            keepdims=True,
        )
    tiles[y, z // 8, z % 8, 5, pl.ds(rank8, 1)] = jnp.concatenate([pair[0:1], pair[1:2]], axis=1)

    def to_z(dz, carry):
        mine = tiles.at[y, z // 8, z % 8, :, pl.ds(rank8, 1)]
        pltpu.make_async_remote_copy(
            mine,
            mine,
            z_out,
            z_in,
            device_id={"curve": place(y, (z + dz) % NZ, c)},
            device_id_type=MESH,
        ).start()
        return carry

    lax.fori_loop(1, NZ, to_z, 0)
    lax.fori_loop(FIRST, PEERS - 1, send_block, 0)

    leaf_moments[...] = dot_left(
        held, ones_where(iota((LEAVES_DEV, 256), 0) == cell), NT
    )[:TERMS]
    leaf_copy = pltpu.make_async_copy(leaf_moments, leaf_hbm, leaf_sem)
    leaf_copy.start()

    pltpu.make_async_copy(z_size, z_size, z_in).wait()

    def spread_tiles(along_y, along_x, turn):
        for step in range(1, NY):
            pltpu.make_async_remote_copy(
                along_y,
                along_y,
                gather_out.at[turn],
                gather_in.at[turn],
                device_id={"curve": place((y + step) % NY, z, c)},
                device_id_type=MESH,
            ).start()
            pltpu.make_async_remote_copy(
                along_x,
                along_x,
                gather_out.at[turn + 1],
                gather_in.at[turn + 1],
                device_id={"rep": (x + step) % NX},
                device_id_type=MESH,
            ).start()

    spread_tiles(
        tiles.at[y, 0, :, :, pl.ds(rank8, 1)],
        tiles.at[y, 1, :, :, pl.ds(rank8, 1)],
        0,
    )
    small = tiles.at[pl.ds(0, 3), 0, :, :, pl.ds(0, 1)]
    pltpu.make_async_copy(small, small, gather_in.at[0]).wait()
    pltpu.make_async_copy(small, small, gather_in.at[1]).wait()
    spread_tiles(
        tiles.at[y, 1, :, :, pl.ds(c * NX, NX)],
        tiles.at[:, 0, :, :, pl.ds(rank8, 1)],
        2,
    )
    large_y = tiles.at[pl.ds(0, 3), 1, :, :, pl.ds(0, 4)]
    large_x = tiles.at[pl.ds(0, 3), 0, :, :, pl.ds(0, 4)]
    pltpu.make_async_copy(large_y, large_y, gather_in.at[2]).wait()
    pltpu.make_async_copy(large_x, large_x, gather_in.at[3]).wait()
    half = tiles.at[:, :, :, :, pl.ds(c * NX, NX)]
    swap = pltpu.make_async_remote_copy(
        half,
        half,
        core_out,
        core_in,
        device_id={"curve": place(y, z, 1 - c)},
        device_id_type=MESH,
    )
    swap.start()
    swap.wait_recv()

    def write_column(index, carry):
        at = pl.ds(pl.multiple_of(index * 128, 128), 128)
        for row in range(5):
            whole = turn_blocks(tiles[index // 16, (index // 8) % 2, index % 8, row])
            if row < 4:
                tree[8 * row : 8 * row + 8, at] = whole
            else:
                tree[32:35, at] = whole[:3]
        return carry

    lax.fori_loop(0, NY * NZ, write_column, 0)
    pairs = jnp.transpose(tiles[:, :, :, 5].reshape(512, 128))
    stacked = jnp.concatenate(
        [
            jnp.concatenate(
                [pairs[:ROWS, 64 * j : 64 * j + 64], pairs[64 : 64 + ROWS, 64 * j : 64 * j + 64]],
                axis=1,
            )
            for j in range(8)
        ],
        axis=0,
    )
    wide = iota((128, 128), 0)
    thin = iota((128, 128), 1)
    folded = dot_left(stacked, ones_where(2 * (wide % 64) + wide // 64 == thin))
    whole_three = jnp.concatenate([folded[j * ROWS : (j + 1) * ROWS] for j in range(8)], axis=1)
    tree[:, 8192:9216] = whole_three[:TERMS]
    four = raise_by(table, whole_three, iota((1, 1024), 1) % 8)
    eight = iota((1024, 128), 0) // 8 == iota((1024, 128), 1)
    tree[:, 9216:9344] = dot_left(four, ones_where(eight))[:TERMS]
    tree_copy = pltpu.make_async_copy(tree, tree_hbm, tree_sem)
    tree_copy.start()

    pltpu.make_async_copy(landed, landed, bulk_in).wait()
    pltpu.make_async_copy(bulk_size, bulk_size, bulk_out).wait()
    pltpu.make_async_copy(slip_size, slip_size, slip_out).wait()
    pltpu.make_async_copy(z_size, z_size, z_out).wait()
    pltpu.make_async_copy(small, small, gather_out.at[0]).wait()
    pltpu.make_async_copy(small, small, gather_out.at[1]).wait()
    pltpu.make_async_copy(large_y, large_y, gather_out.at[2]).wait()
    pltpu.make_async_copy(large_x, large_x, gather_out.at[3]).wait()
    swap.wait_send()
    leaf_copy.wait()
    tree_copy.wait()


def store(
    landed,
    leaf_moments,
    tree,
    places,
    weights,
    leaf_out,
    tree_out,
    landed_kept,
    leaf_kept,
    tree_kept,
    in_sems,
    out_sems,
):
    steps = [(landed.at[p], landed_kept.at[p], places.at[p]) for p in range(3)]
    steps.append((landed.at[3], landed_kept.at[3], weights))
    for part in range(5):
        rows = pl.ds(8 * part, 8 if part < 4 else 3)
        steps.append((tree.at[rows], tree_kept.at[rows], tree_out.at[rows]))
    steps.append((leaf_moments, leaf_kept, leaf_out))
    ins = [
        pltpu.make_async_copy(source, kept, in_sems.at[index])
        for index, (source, kept, _) in enumerate(steps)
    ]
    outs = [
        pltpu.make_async_copy(kept, target, out_sems.at[index])
        for index, (_, kept, target) in enumerate(steps)
    ]
    for copy in ins:
        copy.start()
    for first, second in zip(ins, outs):
        first.wait()
        second.start()
    for copy in outs:
        copy.wait()


def shards(offsets, masses, destination, leaf_ids):
    landed, leaf_moments, tree = pl.pallas_call(
        exchange,
        out_shape=(
            jax.ShapeDtypeStruct((4, 256, 256), jnp.float32),
            jax.ShapeDtypeStruct((TERMS, LEAVES_DEV), jnp.float32),
            jax.ShapeDtypeStruct((TERMS, 9344), jnp.float32),
        ),
        in_specs=[pl.BlockSpec(memory_space=pltpu.HBM)] * 6,
        out_specs=(pl.BlockSpec(memory_space=pl.ANY),) * 3,
        scratch_shapes=[
            pltpu.VMEM((3, 128, 256), jnp.float32),
            pltpu.VMEM((128, 256), jnp.float32),
            pltpu.VMEM((1, 128), jnp.int32),
            pltpu.VMEM((1, 128), jnp.int32),
            pltpu.VMEM((8 * ROWS, ROWS), jnp.float32),
            pltpu.VMEM((64, TERMS * 8), jnp.float32),
            pltpu.VMEM((PEERS - 1, 8, 256), jnp.float32),
            pltpu.VMEM((PEERS - 1, 1, 128), jnp.float32),
            pltpu.SemaphoreType.DMA((6,)),
            pltpu.VMEM((4, 256, 256), jnp.float32),
            pltpu.VMEM((PEERS, 128), jnp.float32),
            pltpu.VMEM((PEERS, 128), jnp.float32),
            pltpu.VMEM((TERMS, LEAVES_DEV), jnp.float32),
            pltpu.VMEM((TERMS, 9344), jnp.float32),
            pltpu.VMEM((NY, 2, 8, TILE_ROWS, 8, 128), jnp.float32),
            pltpu.VMEM(((NZ - 1) * TILE_ROWS, 1, 128), jnp.float32),
            pltpu.SemaphoreType.REGULAR,
        ]
        + [pltpu.SemaphoreType.DMA] * 8
        + [pltpu.SemaphoreType.DMA((4,))] * 2
        + [pltpu.SemaphoreType.DMA] * 2,
        compiler_params=pltpu.CompilerParams(
            collective_id=1, has_side_effects=True, vmem_limit_bytes=60 * 1024 * 1024
        ),
        name="exchange",
    )(
        jnp.transpose(offsets, (1, 0, 2)),
        masses,
        destination.reshape(1, 128),
        leaf_ids.reshape(1, 128),
        jnp.asarray(octant_table()),
        jnp.asarray(fold_table()),
    )
    places, weights, leaf_moments, tree = pl.pallas_call(
        store,
        out_shape=(
            jax.ShapeDtypeStruct((3, 256, 256), jnp.float32),
            jax.ShapeDtypeStruct((256, 256), jnp.float32),
            jax.ShapeDtypeStruct((TERMS, LEAVES_DEV), jnp.float32),
            jax.ShapeDtypeStruct((TERMS, 9344), jnp.float32),
        ),
        in_specs=[pl.BlockSpec(memory_space=pl.ANY)] * 3,
        out_specs=(pl.BlockSpec(memory_space=pl.ANY),) * 4,
        scratch_shapes=[
            pltpu.VMEM((4, 256, 256), jnp.float32),
            pltpu.VMEM((TERMS, LEAVES_DEV), jnp.float32),
            pltpu.VMEM((TERMS, 9344), jnp.float32),
            pltpu.SemaphoreType.DMA((10,)),
            pltpu.SemaphoreType.DMA((10,)),
        ],
        compiler_params=pltpu.CompilerParams(vmem_limit_bytes=60 * 1024 * 1024),
        name="store",
    )(landed, leaf_moments, tree)
    return jnp.transpose(places, (1, 0, 2)), weights, leaf_moments, tree


def solution(mesh):
    placed = (
        P(("curve", "rep"), None, None),
        P(("curve", "rep"), None),
        P(("curve", "rep"), None),
        P(("curve", "rep")),
    )
    return jax.shard_map(
        shards,
        mesh=mesh,
        in_specs=placed,
        out_specs=(
            P(("curve", "rep"), None, None),
            P(("curve", "rep"), None),
            P(None, ("curve", "rep")),
            P(),
        ),
        check_vma=False,
    )
```

time: 345 us -> 80.5 us (0.23)
  waiting for transfers between devices: 165 us -> 0 us
  blocking collectives: 93.4 us -> 0 us
  Pallas kernels: 0 us -> 79.7 us
  starting transfers between devices: 34.6 us -> 0 us
  local copies, waits for them, and re-layouts: 21.3 us -> 0 us
  between operations: 14.3 us -> 0.64 us
  matrix products: 9.74 us -> 0 us
  other arithmetic: 5.25 us -> 0 us
    all_gather x1 -> x0, waiting for transfers between devices: 94.3 us -> none  [shards(): whole_two = lax.all_gather(level_two, ('curve', 'rep'), axis=1, tiled=True)]
    all_gather x1 -> x0, blocking collectives: 85 us -> none  [shards(): level_three = lax.all_gather(group_three, 'curve', axis=1, tiled=True)]
    pallas_call x0 -> x2, Pallas kernels: none -> 79.7 us  [the longest x1 77.1 us: shards(): pl.pallas_call(exchange, out_shape=(jax.ShapeDtypeStruct((4, 256, 256), j...]
    all_to_all x3 -> x0, waiting for transfers between devices: 70.9 us -> none  [the longest x1 41.7 us: shards(): lax.all_to_all(send_places, 'curve', split_axis=0, concat_axis=0, tiled=T...]
    all_to_all x3 -> x0, starting transfers between devices: 34.4 us -> none  [the longest x1 20.6 us: shards(): lax.all_to_all(send_leaves, 'curve', split_axis=0, concat_axis=0, tiled=T...]
    dot_general x9 -> x0, matrix products: 9.74 us -> none  [the longest x4 6.92 us: block_group(): jnp.einsum('agp,kgp->gak', xstack, yzstack, precision=lax.Precision.HIGHEST)]
    psum x1 -> x0, blocking collectives: 8.49 us -> none  [shards(): group_three = lax.psum(partial_three, 'rep')]
    scatter x3 -> x0, local copies, waits for them, and re-layouts: 6.91 us -> none  [the longest x1 4.36 us: shards(): send_places = jnp.zeros((total, 3, points), jnp.float32).at[slot_index].s...]
  transfers between devices with their start and end apart: 4 -> 0, of which waited for: 4 -> 0; matrix products, arithmetic and copies ran while one was open for 4% -> 0% of each run, Pallas kernels for 0% -> 0%
where the time goes in v1:
time: 80.5 us; the launch traced here: 80.3 us
  Pallas kernels  79.7 us (99%)
    pallas_call x1, Pallas kernels, shards(): pl.pallas_call(exchange, out_shape=(jax.ShapeDtypeStruct((4, 256, 256), j...  77.1 us
    pallas_call x1, Pallas kernels, shards(): pl.pallas_call(store, out_shape=(jax.ShapeDtypeStruct((3, 256, 256), jnp....  2.63 us

profile of v1, /device:TPU:1, one launch (start us, length us, event | category | flops | bytes accessed | tf_op | source)
XLA Modules:
  0.0 80.3 jit_solution(7661682426684982379)
XLA Ops:
  0.6 77.1 %exchange.1 = (f32[4,256,256]{2,1,0:T(8,128)}, f32[35,1024]{1,0:T(8,128)}, f32[35,9344]{1,0:T(8,128)}) custom-call(f32[3,128,256]{2,1,0:T(8,128)} %bitcast.4, f32[128,256]{1,0:T(8,128)} %masses_hbm.1, s32[1,128]{1,0:T(1,128)} %bitcast.5, s32[1,128]{1,0:T(1,128)} %bitcast.6, f32[320,40]{1,0:T(8,128)} %constant.4.clone.table_hbm, f32[64,280]{1,0:T(8,128)} %constant.5.clone.fold_hbm), custom_call_target="tpu_custom_call" | custom-call | tf_op jit(solution)/shard_map/exchange/pallas_call | solution.py:477
  77.7 2.6 %store.1 = (f32[3,256,256]{2,1,0:T(8,128)}, f32[256,256]{1,0:T(8,128)}, f32[35,1024]{1,0:T(8,128)}, f32[35,9344]{1,0:T(8,128)}) custom-call(f32[4,256,256]{2,1,0:T(8,128)} %get-tuple-element.11.landed, f32[35,1024]{1,0:T(8,128)} %get-tuple-element.12.leaf_moments, f32[35,9344]{1,0:T(8,128)} %get-tuple-element.13.tree), custom_call_target="tpu_custom_call" | custom-call | tf_op jit(solution)/shard_map/store/pallas_call | solution.py:520

commit v2 on v1

--- a/solution.py
+++ b/solution.py
@@ -15,8 +15,7 @@
 LEAVES_DEV = 1024
 TERMS = 35
 ROWS = 40
-TILE_ROWS = 6
-FIRST = 16
+TILE_ROWS = 7
 
 
 def moment_terms():
@@ -28,25 +27,6 @@
     return listed
 
 
-def octant_table():
-    listed = moment_terms()
-    table = np.zeros((8, ROWS, ROWS), dtype=np.float32)
-    for octant in range(8):
-        signs = (2 * (octant % 2) - 1, 2 * (octant // 2 % 2) - 1, 2 * (octant // 4) - 1)
-        for row, upper in enumerate(listed):
-            for column, lower in enumerate(listed):
-                if all(lower[i] <= upper[i] for i in range(3)):
-                    value = 0.125 * 2.0 ** (-sum(upper))
-                    for i in range(3):
-                        value = (
-                            value
-                            * math.comb(upper[i], lower[i])
-                            * signs[i] ** (upper[i] - lower[i])
-                        )
-                    table[octant, row, column] = value
-    return table.reshape(8 * ROWS, ROWS)
-
-
 def fold_table():
     table = np.zeros((64, TERMS * 8), dtype=np.float32)
     for term in range(TERMS):
@@ -88,12 +68,37 @@
     return jnp.where(mask, 1.0, 0.0).astype(jnp.bfloat16)
 
 
-def raise_by(table, value, octant):
-    moved = dot_right(table, value)
-    total = jnp.zeros_like(value)
-    for g in range(8):
-        total = total + jnp.where(octant == g, moved[g * ROWS : (g + 1) * ROWS], 0.0)
-    return total
+def signs(cell, levels):
+    found = []
+    for axis in range(3):
+        total = None
+        for level in range(levels):
+            sign = 2 * ((cell >> (3 * level + axis)) & 1) - 1
+            total = sign if level == 0 else total + (sign << level)
+        found.append(total.astype(jnp.float32))
+    return found
+
+
+def lifted(rows, offsets, levels):
+    listed = moment_terms()
+    held = dict(zip(listed, rows))
+    for axis in range(3):
+        powers = [None, offsets[axis]]
+        for _ in range(3):
+            powers.append(powers[-1] * offsets[axis])
+        factors = {}
+        made = {}
+        for term in listed:
+            total = held[term]
+            for step in range(1, term[axis] + 1):
+                kind = (term[axis], step)
+                if kind not in factors:
+                    factors[kind] = powers[step] * float(math.comb(term[axis], step))
+                lower = tuple(n - (step if i == axis else 0) for i, n in enumerate(term))
+                total = total + factors[kind] * held[lower]
+            made[term] = total
+        held = made
+    return [held[term] * (0.125**levels * 0.5 ** (levels * sum(term))) for term in listed]
 
 
 def particle_moments(planes, fold):
@@ -131,16 +136,14 @@
     masses_hbm,
     target_hbm,
     leaves_hbm,
-    table_hbm,
     fold_hbm,
     landed,
-    leaf_hbm,
-    tree_hbm,
+    leaf_moments,
+    tree,
     offsets,
     masses,
     target,
     leaves,
-    table_ref,
     fold_ref,
     bulk_size,
     slip_size,
@@ -148,13 +151,11 @@
     packed,
     slips,
     got_slips,
-    leaf_moments,
-    tree,
+    turned,
+    raised,
     tiles,
     z_size,
     ready,
-    leaf_sem,
-    tree_sem,
     slip_out,
     slip_in,
     bulk_out,
@@ -183,7 +184,6 @@
                 (masses_hbm, masses),
                 (offsets_hbm, offsets),
                 (fold_hbm, fold_ref),
-                (table_hbm, table_ref),
             )
         )
     ]
@@ -219,7 +219,6 @@
     for load in loads:
         load.wait()
 
-    table = table_ref[...].astype(jnp.bfloat16)
     aim = target[...]
     leaf = leaves[...]
     named = ones_where(iota((PEERS, 128), 0) == aim)
@@ -256,15 +255,11 @@
     for index, plane in enumerate(planes):
         packed[index] = dot_right(spread, plane)
 
-    pl.semaphore_wait(ready, 7)
-
-    def peer(step):
-        turn, inner = step // 8, 7 - step % 8
-        dz = NZ // 2 + (1 - turn % 2) * (turn // 2) - (turn % 2) * ((turn + 1) // 2)
+    def peer(step, inner):
+        dz = NZ // 2 + (1 - step % 2) * (step // 2) - (step % 2) * ((step + 1) // 2)
         return place((y + inner // 2) % NY, (z + dz) % NZ, (c + inner % 2) % 2)
 
-    def send_slip(step, carry):
-        to = peer(step)
+    def send_slip(to):
         pltpu.make_async_remote_copy(
             slips.at[pl.ds(to, 1)],
             got_slips.at[pl.ds(me, 1)],
@@ -273,15 +268,8 @@
             device_id={"curve": to},
             device_id_type=MESH,
         ).start()
-        return carry
-
-    lax.fori_loop(0, PEERS - 1, send_slip, 0)
-    pltpu.make_async_copy(
-        slips.at[pl.ds(me, 1)], got_slips.at[pl.ds(me, 1)], slip_in
-    ).start()
-
-    def send_block(step, carry):
-        to = peer(step)
+
+    def send_block(to):
         pltpu.make_async_remote_copy(
             packed.at[:, pl.ds(2 * to, 2)],
             landed.at[:, pl.ds(2 * me, 2)],
@@ -290,26 +278,52 @@
             device_id={"curve": to},
             device_id_type=MESH,
         ).start()
-        return carry
-
-    lax.fori_loop(0, FIRST, send_block, 0)
+
+    def along_z(send):
+        def body(step, carry):
+            send(peer(step, 0))
+            return carry
+
+        lax.fori_loop(0, NZ - 1, body, 0)
+
+    def all_others(send):
+        def body(step, carry):
+            send(peer(step // 7, 7 - step % 7))
+            return carry
+
+        lax.fori_loop(0, 7 * NZ, body, 0)
+
+    along_z(send_slip)
+    pl.semaphore_wait(ready, 7)
+    all_others(send_slip)
+    along_z(send_block)
+    pltpu.make_async_copy(
+        slips.at[pl.ds(me, 1)], got_slips.at[pl.ds(me, 1)], slip_in
+    ).start()
+
     pltpu.make_async_copy(
         packed.at[:, pl.ds(2 * me, 2)], landed.at[:, pl.ds(2 * me, 2)], bulk_in
     ).start()
 
     pltpu.make_async_copy(got_slips, got_slips, slip_in).wait()
-    turned = jnp.transpose(got_slips[...])
-    held = jnp.concatenate([turned[:ROWS], turned[64 : 64 + ROWS]], axis=1)
-    cell = held[TERMS : TERMS + 1].astype(jnp.int32)
-    one = raise_by(table, held, cell & 7)
-    two = raise_by(table, one, (cell >> 3) & 7)
-    three = raise_by(table, two, (cell >> 6) & 7)
-    level_two = dot_left(two, ones_where(iota((128, 256), 0) % 16 == cell >> 6), NT)
-    pair = dot_right(
-        ones_where(iota((8, 256), 0) == cell >> 9),
-        jnp.concatenate([three, jnp.zeros((64 - ROWS, 256), jnp.float32)], axis=0),
-        NT,
-    )
+    turned[...] = jnp.transpose(got_slips[...])
+    cell = jnp.concatenate(
+        [turned[TERMS : TERMS + 1], turned[64 + TERMS : 65 + TERMS]], axis=1
+    ).astype(jnp.int32)
+    rows = [
+        jnp.concatenate([turned[r : r + 1], turned[64 + r : 65 + r]], axis=1)
+        for r in range(TERMS)
+    ]
+    raised[...] = jnp.zeros_like(raised)
+    whole_cell = cell + 1024 * x
+    for first, levels in ((0, 2), (64, 3), (128, 4)):
+        for r, row in enumerate(lifted(rows, signs(whole_cell, levels), levels)):
+            raised[first + r : first + r + 1] = row
+    level_two = dot_left(
+        raised[0:ROWS], ones_where(iota((128, 256), 0) % 16 == cell >> 6), NT
+    )
+    kind = iota((8, 256), 0)
+    upper = dot_right(ones_where((kind == cell >> 9) | (kind == 2)), raised[64:192], NT)
     own_lanes = iota((8, 128), 1) // 16 == iota((8, 128), 0)
     for row in range(5):
         tiles[y, z // 8, z % 8, row, pl.ds(rank8, 1)] = jnp.sum(
@@ -317,7 +331,10 @@
             axis=0,
             keepdims=True,
         )
-    tiles[y, z // 8, z % 8, 5, pl.ds(rank8, 1)] = jnp.concatenate([pair[0:1], pair[1:2]], axis=1)
+    tiles[y, z // 8, z % 8, 5, pl.ds(rank8, 1)] = jnp.concatenate(
+        [upper[0:1, :64], upper[1:2, :64]], axis=1
+    )
+    tiles[y, z // 8, z % 8, 6, pl.ds(rank8, 1)] = upper[2:3]
 
     def to_z(dz, carry):
         mine = tiles.at[y, z // 8, z % 8, :, pl.ds(rank8, 1)]
@@ -332,13 +349,12 @@
         return carry
 
     lax.fori_loop(1, NZ, to_z, 0)
-    lax.fori_loop(FIRST, PEERS - 1, send_block, 0)
-
+    all_others(send_block)
+
+    held = jnp.concatenate([turned[:ROWS], turned[64 : 64 + ROWS]], axis=1)
     leaf_moments[...] = dot_left(
         held, ones_where(iota((LEAVES_DEV, 256), 0) == cell), NT
     )[:TERMS]
-    leaf_copy = pltpu.make_async_copy(leaf_moments, leaf_hbm, leaf_sem)
-    leaf_copy.start()
 
     pltpu.make_async_copy(z_size, z_size, z_in).wait()
 
@@ -376,31 +392,39 @@
     )
     large_y = tiles.at[pl.ds(0, 3), 1, :, :, pl.ds(0, 4)]
     large_x = tiles.at[pl.ds(0, 3), 0, :, :, pl.ds(0, 4)]
-    pltpu.make_async_copy(large_y, large_y, gather_in.at[2]).wait()
     pltpu.make_async_copy(large_x, large_x, gather_in.at[3]).wait()
-    half = tiles.at[:, :, :, :, pl.ds(c * NX, NX)]
-    swap = pltpu.make_async_remote_copy(
-        half,
-        half,
-        core_out,
-        core_in,
-        device_id={"curve": place(y, z, 1 - c)},
-        device_id_type=MESH,
-    )
-    swap.start()
-    swap.wait_recv()
-
-    def write_column(index, carry):
-        at = pl.ds(pl.multiple_of(index * 128, 128), 128)
-        for row in range(5):
-            whole = turn_blocks(tiles[index // 16, (index // 8) % 2, index % 8, row])
-            if row < 4:
-                tree[8 * row : 8 * row + 8, at] = whole
-            else:
-                tree[32:35, at] = whole[:3]
-        return carry
-
-    lax.fori_loop(0, NY * NZ, write_column, 0)
+    swaps = []
+    for half in range(2):
+        if half:
+            pltpu.make_async_copy(large_y, large_y, gather_in.at[2]).wait()
+        mine = tiles.at[:, half, :, :, pl.ds(c * NX, NX)]
+        swap = pltpu.make_async_remote_copy(
+            mine,
+            mine,
+            core_out.at[half],
+            core_in.at[half],
+            device_id={"curve": place(y, z, 1 - c)},
+            device_id_type=MESH,
+        )
+        swap.start()
+        swaps.append(swap)
+
+    for half in range(2):
+        swaps[half].wait_recv()
+
+        def write_column(index, carry, half=half):
+            at_y, at_z = index // 8, index % 8
+            column = at_y * NZ + half * 8 + at_z
+            at = pl.ds(pl.multiple_of(column * 128, 128), 128)
+            for row in range(5):
+                whole = turn_blocks(tiles[at_y, half, at_z, row])
+                if row < 4:
+                    tree[8 * row : 8 * row + 8, at] = whole
+                else:
+                    tree[32:35, at] = whole[:3]
+            return carry
+
+        lax.fori_loop(0, NY * 8, write_column, 0)
     pairs = jnp.transpose(tiles[:, :, :, 5].reshape(512, 128))
     stacked = jnp.concatenate(
         [
@@ -417,12 +441,9 @@
     folded = dot_left(stacked, ones_where(2 * (wide % 64) + wide // 64 == thin))
     whole_three = jnp.concatenate([folded[j * ROWS : (j + 1) * ROWS] for j in range(8)], axis=1)
     tree[:, 8192:9216] = whole_three[:TERMS]
-    four = raise_by(table, whole_three, iota((1, 1024), 1) % 8)
-    eight = iota((1024, 128), 0) // 8 == iota((1024, 128), 1)
-    tree[:, 9216:9344] = dot_left(four, ones_where(eight))[:TERMS]
-    tree_copy = pltpu.make_async_copy(tree, tree_hbm, tree_sem)
-    tree_copy.start()
-
+    tops = jnp.transpose(tiles[:, :, :, 6].reshape(512, 128))[64 : 64 + ROWS]
+    four = iota((512, 128), 0) // 4 == iota((512, 128), 1)
+    tree[:, 9216:9344] = dot_left(tops, ones_where(four))[:TERMS]
     pltpu.make_async_copy(landed, landed, bulk_in).wait()
     pltpu.make_async_copy(bulk_size, bulk_size, bulk_out).wait()
     pltpu.make_async_copy(slip_size, slip_size, slip_out).wait()
@@ -431,49 +452,36 @@
     pltpu.make_async_copy(small, small, gather_out.at[1]).wait()
     pltpu.make_async_copy(large_y, large_y, gather_out.at[2]).wait()
     pltpu.make_async_copy(large_x, large_x, gather_out.at[3]).wait()
-    swap.wait_send()
-    leaf_copy.wait()
-    tree_copy.wait()
-
-
-def store(
-    landed,
-    leaf_moments,
-    tree,
-    places,
-    weights,
-    leaf_out,
-    tree_out,
-    landed_kept,
-    leaf_kept,
-    tree_kept,
-    in_sems,
-    out_sems,
-):
-    steps = [(landed.at[p], landed_kept.at[p], places.at[p]) for p in range(3)]
-    steps.append((landed.at[3], landed_kept.at[3], weights))
+    for swap in swaps:
+        swap.wait_send()
+
+
+def store(landed, leaf_moments, tree, places, weights, leaf_out, tree_out, sems):
+    steps = [(landed.at[p], places.at[p]) for p in range(3)]
+    steps.append((landed.at[3], weights))
     for part in range(5):
         rows = pl.ds(8 * part, 8 if part < 4 else 3)
-        steps.append((tree.at[rows], tree_kept.at[rows], tree_out.at[rows]))
-    steps.append((leaf_moments, leaf_kept, leaf_out))
-    ins = [
-        pltpu.make_async_copy(source, kept, in_sems.at[index])
-        for index, (source, kept, _) in enumerate(steps)
+        steps.append((tree.at[rows], tree_out.at[rows]))
+    steps.append((leaf_moments, leaf_out))
+    copies = [
+        pltpu.make_async_copy(kept, target, sems.at[index])
+        for index, (kept, target) in enumerate(steps)
     ]
-    outs = [
-        pltpu.make_async_copy(kept, target, out_sems.at[index])
-        for index, (_, kept, target) in enumerate(steps)
-    ]
-    for copy in ins:
+    for copy in copies:
         copy.start()
-    for first, second in zip(ins, outs):
-        first.wait()
-        second.start()
-    for copy in outs:
+    for copy in copies:
         copy.wait()
 
 
 def shards(offsets, masses, destination, leaf_ids):
+    vmem = pl.BlockSpec(memory_space=pltpu.VMEM)
+    operands = (
+        jnp.transpose(offsets, (1, 0, 2)),
+        masses,
+        destination.reshape(1, 128),
+        leaf_ids.reshape(1, 128),
+        jnp.asarray(fold_table()),
+    )
     landed, leaf_moments, tree = pl.pallas_call(
         exchange,
         out_shape=(
@@ -481,42 +489,34 @@
             jax.ShapeDtypeStruct((TERMS, LEAVES_DEV), jnp.float32),
             jax.ShapeDtypeStruct((TERMS, 9344), jnp.float32),
         ),
-        in_specs=[pl.BlockSpec(memory_space=pltpu.HBM)] * 6,
-        out_specs=(pl.BlockSpec(memory_space=pl.ANY),) * 3,
+        in_specs=[pl.BlockSpec(memory_space=pltpu.HBM)] * 5,
+        out_specs=(vmem,) * 3,
         scratch_shapes=[
             pltpu.VMEM((3, 128, 256), jnp.float32),
             pltpu.VMEM((128, 256), jnp.float32),
             pltpu.VMEM((1, 128), jnp.int32),
             pltpu.VMEM((1, 128), jnp.int32),
-            pltpu.VMEM((8 * ROWS, ROWS), jnp.float32),
             pltpu.VMEM((64, TERMS * 8), jnp.float32),
             pltpu.VMEM((PEERS - 1, 8, 256), jnp.float32),
             pltpu.VMEM((PEERS - 1, 1, 128), jnp.float32),
-            pltpu.SemaphoreType.DMA((6,)),
+            pltpu.SemaphoreType.DMA((5,)),
             pltpu.VMEM((4, 256, 256), jnp.float32),
             pltpu.VMEM((PEERS, 128), jnp.float32),
             pltpu.VMEM((PEERS, 128), jnp.float32),
-            pltpu.VMEM((TERMS, LEAVES_DEV), jnp.float32),
-            pltpu.VMEM((TERMS, 9344), jnp.float32),
+            pltpu.VMEM((PEERS, 128), jnp.float32),
+            pltpu.VMEM((192, 256), jnp.float32),
             pltpu.VMEM((NY, 2, 8, TILE_ROWS, 8, 128), jnp.float32),
             pltpu.VMEM(((NZ - 1) * TILE_ROWS, 1, 128), jnp.float32),
             pltpu.SemaphoreType.REGULAR,
         ]
-        + [pltpu.SemaphoreType.DMA] * 8
+        + [pltpu.SemaphoreType.DMA] * 6
         + [pltpu.SemaphoreType.DMA((4,))] * 2
-        + [pltpu.SemaphoreType.DMA] * 2,
+        + [pltpu.SemaphoreType.DMA((2,))] * 2,
         compiler_params=pltpu.CompilerParams(
-            collective_id=1, has_side_effects=True, vmem_limit_bytes=60 * 1024 * 1024
+            collective_id=1, has_side_effects=True, vmem_limit_bytes=40 * 1024 * 1024
         ),
         name="exchange",
-    )(
-        jnp.transpose(offsets, (1, 0, 2)),
-        masses,
-        destination.reshape(1, 128),
-        leaf_ids.reshape(1, 128),
-        jnp.asarray(octant_table()),
-        jnp.asarray(fold_table()),
-    )
+    )(*[pltpu.with_memory_space_constraint(operand, pltpu.HBM) for operand in operands])
     places, weights, leaf_moments, tree = pl.pallas_call(
         store,
         out_shape=(
@@ -525,16 +525,10 @@
             jax.ShapeDtypeStruct((TERMS, LEAVES_DEV), jnp.float32),
             jax.ShapeDtypeStruct((TERMS, 9344), jnp.float32),
         ),
-        in_specs=[pl.BlockSpec(memory_space=pl.ANY)] * 3,
+        in_specs=[vmem] * 3,
         out_specs=(pl.BlockSpec(memory_space=pl.ANY),) * 4,
-        scratch_shapes=[
-            pltpu.VMEM((4, 256, 256), jnp.float32),
-            pltpu.VMEM((TERMS, LEAVES_DEV), jnp.float32),
-            pltpu.VMEM((TERMS, 9344), jnp.float32),
-            pltpu.SemaphoreType.DMA((10,)),
-            pltpu.SemaphoreType.DMA((10,)),
-        ],
-        compiler_params=pltpu.CompilerParams(vmem_limit_bytes=60 * 1024 * 1024),
+        scratch_shapes=[pltpu.SemaphoreType.DMA((10,))],
+        compiler_params=pltpu.CompilerParams(vmem_limit_bytes=40 * 1024 * 1024),
         name="store",
     )(landed, leaf_moments, tree)
     return jnp.transpose(places, (1, 0, 2)), weights, leaf_moments, tree

time: 80.5 us -> 76.1 us (0.945)
  Pallas kernels: 79.7 us -> 75.4 us
    pallas_call x1, Pallas kernels: 77.1 us -> 73.8 us  [shards(): pl.pallas_call(exchange, out_shape=(jax.ShapeDtypeStruct((4, 256, 256), j...]
    pallas_call x1, Pallas kernels: 2.63 us -> 1.59 us  [shards(): pl.pallas_call(store, out_shape=(jax.ShapeDtypeStruct((3, 256, 256), jnp....]
where the time goes in v2:
time: 76.1 us; the launch traced here: 76 us
  Pallas kernels  75.4 us (99%)
    pallas_call x1, Pallas kernels, shards(): pl.pallas_call(exchange, out_shape=(jax.ShapeDtypeStruct((4, 256, 256), j...  73.8 us
    pallas_call x1, Pallas kernels, shards(): pl.pallas_call(store, out_shape=(jax.ShapeDtypeStruct((3, 256, 256), jnp....  1.59 us

profile of v2, /device:TPU:1, one launch (start us, length us, event | category | flops | bytes accessed | tf_op | source)
XLA Modules:
  0.0 76.0 jit_solution(15938449163357345724)
XLA Ops:
  0.6 73.8 %exchange.1 = (f32[4,256,256]{2,1,0:T(8,128)S(1)}, f32[35,1024]{1,0:T(8,128)S(1)}, f32[35,9344]{1,0:T(8,128)S(1)}) custom-call(f32[3,128,256]{2,1,0:T(8,128)} %bitcast.4, f32[128,256]{1,0:T(8,128)} %masses_hbm.1, s32[1,128]{1,0:T(1,128)} %bitcast.5, s32[1,128]{1,0:T(1,128)} %bitcast.6, f32[64,280]{1,0:T(8,128)} %constant.2.clone.fold_hbm), custom_call_target="tpu_custom_call" | custom-call | tf_op jit(solution)/shard_map/exchange/pallas_call | solution.py:485
  74.4 1.6 %store.1 = (f32[3,256,256]{2,1,0:T(8,128)}, f32[256,256]{1,0:T(8,128)}, f32[35,1024]{1,0:T(8,128)}, f32[35,9344]{1,0:T(8,128)}) custom-call(f32[4,256,256]{2,1,0:T(8,128)S(1)} %get-tuple-element.11.landed, f32[35,1024]{1,0:T(8,128)S(1)} %get-tuple-element.12.leaf_moments, f32[35,9344]{1,0:T(8,128)S(1)} %get-tuple-element.13.tree), custom_call_target="tpu_custom_call" | custom-call | tf_op jit(solution)/shard_map/store/pallas_call | solution.py:520

commit v3 on v2

--- a/solution.py
+++ b/solution.py
@@ -15,7 +15,8 @@
 LEAVES_DEV = 1024
 TERMS = 35
 ROWS = 40
-TILE_ROWS = 7
+SPARE = 48
+TILE_ROWS = 5
 
 
 def moment_terms():
@@ -315,26 +316,30 @@
         for r in range(TERMS)
     ]
     raised[...] = jnp.zeros_like(raised)
-    whole_cell = cell + 1024 * x
-    for first, levels in ((0, 2), (64, 3), (128, 4)):
-        for r, row in enumerate(lifted(rows, signs(whole_cell, levels), levels)):
+    for r, row in enumerate(lifted(rows, signs(cell, 2), 2)):
+        raised[r : r + 1] = row
+    for r, row in enumerate(lifted(rows, signs(cell, 3), 3)):
+        for first in (64 + SPARE, 64 + SPARE + TERMS):
             raised[first + r : first + r + 1] = row
     level_two = dot_left(
         raised[0:ROWS], ones_where(iota((128, 256), 0) % 16 == cell >> 6), NT
     )
-    kind = iota((8, 256), 0)
-    upper = dot_right(ones_where((kind == cell >> 9) | (kind == 2)), raised[64:192], NT)
+    upper = dot_right(ones_where(iota((8, 256), 0) == cell >> 9), raised[64:192], NT)
     own_lanes = iota((8, 128), 1) // 16 == iota((8, 128), 0)
-    for row in range(5):
-        tiles[y, z // 8, z % 8, row, pl.ds(rank8, 1)] = jnp.sum(
+    flat = [
+        jnp.sum(
             jnp.where(own_lanes, level_two[8 * row : 8 * row + 8], 0.0),
             axis=0,
             keepdims=True,
         )
-    tiles[y, z // 8, z % 8, 5, pl.ds(rank8, 1)] = jnp.concatenate(
-        [upper[0:1, :64], upper[1:2, :64]], axis=1
-    )
-    tiles[y, z // 8, z % 8, 6, pl.ds(rank8, 1)] = upper[2:3]
+        for row in range(TILE_ROWS)
+    ]
+    lane = iota((1, 128), 1)
+    flat[4] = jnp.where(
+        lane < SPARE, flat[4], jnp.where(lane < SPARE + TERMS, upper[0:1], upper[1:2])
+    )
+    for row in range(TILE_ROWS):
+        tiles[y, z // 8, z % 8, row, pl.ds(rank8, 1)] = flat[row]
 
     def to_z(dz, carry):
         mine = tiles.at[y, z // 8, z % 8, :, pl.ds(rank8, 1)]
@@ -425,11 +430,14 @@
             return carry
 
         lax.fori_loop(0, NY * 8, write_column, 0)
-    pairs = jnp.transpose(tiles[:, :, :, 5].reshape(512, 128))
+    pairs = jnp.transpose(tiles[:, :, :, 4].reshape(512, 128))
     stacked = jnp.concatenate(
         [
             jnp.concatenate(
-                [pairs[:ROWS, 64 * j : 64 * j + 64], pairs[64 : 64 + ROWS, 64 * j : 64 * j + 64]],
+                [
+                    pairs[SPARE : SPARE + ROWS, 64 * j : 64 * j + 64],
+                    pairs[SPARE + TERMS : SPARE + TERMS + ROWS, 64 * j : 64 * j + 64],
+                ],
                 axis=1,
             )
             for j in range(8)
@@ -441,9 +449,11 @@
     folded = dot_left(stacked, ones_where(2 * (wide % 64) + wide // 64 == thin))
     whole_three = jnp.concatenate([folded[j * ROWS : (j + 1) * ROWS] for j in range(8)], axis=1)
     tree[:, 8192:9216] = whole_three[:TERMS]
-    tops = jnp.transpose(tiles[:, :, :, 6].reshape(512, 128))[64 : 64 + ROWS]
-    four = iota((512, 128), 0) // 4 == iota((512, 128), 1)
-    tree[:, 9216:9344] = dot_left(tops, ones_where(four))[:TERMS]
+    below = [tree[r : r + 1, 8192:9216] for r in range(TERMS)]
+    four = jnp.concatenate(lifted(below, signs(iota((1, 1024), 1), 1), 1), axis=0)
+    eight = iota((1024, 128), 0) // 8 == iota((1024, 128), 1)
+    tree[:, 9216:9344] = dot_left(four, ones_where(eight))
+
     pltpu.make_async_copy(landed, landed, bulk_in).wait()
     pltpu.make_async_copy(bulk_size, bulk_size, bulk_out).wait()
     pltpu.make_async_copy(slip_size, slip_size, slip_out).wait()

time: 76.1 us -> 75.4 us (level)
  Pallas kernels: 75.4 us -> 74.6 us
    pallas_call x1, Pallas kernels: 73.8 us -> 73 us  [shards(): pl.pallas_call(exchange, out_shape=(jax.ShapeDtypeStruct((4, 256, 256), j...]
where the time goes in v3:
time: 75.4 us; the launch traced here: 75.2 us
  Pallas kernels  74.6 us (99%)
    pallas_call x1, Pallas kernels, shards(): pl.pallas_call(exchange, out_shape=(jax.ShapeDtypeStruct((4, 256, 256), j...  73 us
    pallas_call x1, Pallas kernels, shards(): pl.pallas_call(store, out_shape=(jax.ShapeDtypeStruct((3, 256, 256), jnp....  1.59 us

profile of v3, /device:TPU:1, one launch (start us, length us, event | category | flops | bytes accessed | tf_op | source)
XLA Modules:
  0.0 75.2 jit_solution(18417467379329189240)
XLA Ops:
  0.6 73.0 %exchange.1 = (f32[4,256,256]{2,1,0:T(8,128)S(1)}, f32[35,1024]{1,0:T(8,128)S(1)}, f32[35,9344]{1,0:T(8,128)S(1)}) custom-call(f32[3,128,256]{2,1,0:T(8,128)} %bitcast.4, f32[128,256]{1,0:T(8,128)} %masses_hbm.1, s32[1,128]{1,0:T(1,128)} %bitcast.5, s32[1,128]{1,0:T(1,128)} %bitcast.6, f32[64,280]{1,0:T(8,128)} %constant.2.clone.fold_hbm), custom_call_target="tpu_custom_call" | custom-call | tf_op jit(solution)/shard_map/exchange/pallas_call | solution.py:495
  73.6 1.6 %store.1 = (f32[3,256,256]{2,1,0:T(8,128)}, f32[256,256]{1,0:T(8,128)}, f32[35,1024]{1,0:T(8,128)}, f32[35,9344]{1,0:T(8,128)}) custom-call(f32[4,256,256]{2,1,0:T(8,128)S(1)} %get-tuple-element.11.landed, f32[35,1024]{1,0:T(8,128)S(1)} %get-tuple-element.12.leaf_moments, f32[35,9344]{1,0:T(8,128)S(1)} %get-tuple-element.13.tree), custom_call_target="tpu_custom_call" | custom-call | tf_op jit(solution)/shard_map/store/pallas_call | solution.py:530

commit v4 on v3

--- a/solution.py
+++ b/solution.py
@@ -176,6 +176,32 @@
     def place(py, pz, pc):
         return (py * NZ + pz) * 2 + pc
 
+    barrier = pltpu.get_barrier_semaphore()
+    near = [(dy, dc) for dy in range(NY) for dc in range(2) if dy or dc]
+    for dz in (8, 7, 9, 6, 10, 5, 11, 4, 12, 3, 13, 2, 14, 1, 15):
+        pl.semaphore_signal(
+            barrier,
+            inc=1,
+            device_id={"curve": place(y, (z + dz) % NZ, c)},
+            device_id_type=MESH,
+        )
+    for dy, dc in near:
+        pl.semaphore_signal(
+            barrier,
+            inc=1,
+            device_id={"curve": place((y + dy) % NY, z, (c + dc) % 2)},
+            device_id_type=MESH,
+        )
+    group = [(dx, dc) for dx in range(NX) for dc in range(2) if dx or dc]
+    for dx, dc in group:
+        if dx:
+            pl.semaphore_signal(
+                barrier,
+                inc=1,
+                device_id={"curve": place(y, z, (c + dc) % 2), "rep": (x + dx) % NX},
+                device_id_type=MESH,
+            )
+
     loads = [
         pltpu.make_async_copy(source, kept, load_sems.at[index])
         for index, (source, kept) in enumerate(
@@ -190,32 +216,6 @@
     ]
     for load in loads:
         load.start()
-
-    barrier = pltpu.get_barrier_semaphore()
-    near = [(dy, dc) for dy in range(NY) for dc in range(2) if dy or dc]
-    for dz in range(1, NZ):
-        pl.semaphore_signal(
-            barrier,
-            inc=1,
-            device_id={"curve": place(y, (z + dz) % NZ, c)},
-            device_id_type=MESH,
-        )
-    for dy, dc in near:
-        pl.semaphore_signal(
-            barrier,
-            inc=1,
-            device_id={"curve": place((y + dy) % NY, z, (c + dc) % 2)},
-            device_id_type=MESH,
-        )
-    group = [(dx, dc) for dx in range(NX) for dc in range(2) if dx or dc]
-    for dx, dc in group:
-        if dx:
-            pl.semaphore_signal(
-                barrier,
-                inc=1,
-                device_id={"curve": place(y, z, (c + dc) % 2), "rep": (x + dx) % NX},
-                device_id_type=MESH,
-            )
 
     for load in loads:
         load.wait()
@@ -354,7 +354,11 @@
         return carry
 
     lax.fori_loop(1, NZ, to_z, 0)
-    all_others(send_block)
+    def mixed(step, carry):
+        send_block(peer((step // 7) * 3 % NZ, 7 - step % 7))
+        return carry
+
+    lax.fori_loop(0, 7 * NZ, mixed, 0)
 
     held = jnp.concatenate([turned[:ROWS], turned[64 : 64 + ROWS]], axis=1)
     leaf_moments[...] = dot_left(

time: 75.4 us -> 74.9 us (level)
  no operation moved by 1% of the time
where the time goes in v4:
time: 74.9 us; the launch traced here: 74.7 us
  Pallas kernels  74.1 us (99%)
    pallas_call x1, Pallas kernels, shards(): pl.pallas_call(exchange, out_shape=(jax.ShapeDtypeStruct((4, 256, 256), j...  72.5 us
    pallas_call x1, Pallas kernels, shards(): pl.pallas_call(store, out_shape=(jax.ShapeDtypeStruct((3, 256, 256), jnp....  1.59 us

profile of v4, /device:TPU:1, one launch (start us, length us, event | category | flops | bytes accessed | tf_op | source)
XLA Modules:
  0.0 74.7 jit_solution(17552551728934504821)
XLA Ops:
  0.6 72.5 %exchange.1 = (f32[4,256,256]{2,1,0:T(8,128)S(1)}, f32[35,1024]{1,0:T(8,128)S(1)}, f32[35,9344]{1,0:T(8,128)S(1)}) custom-call(f32[3,128,256]{2,1,0:T(8,128)} %bitcast.4, f32[128,256]{1,0:T(8,128)} %masses_hbm.1, s32[1,128]{1,0:T(1,128)} %bitcast.5, s32[1,128]{1,0:T(1,128)} %bitcast.6, f32[64,280]{1,0:T(8,128)} %constant.2.clone.fold_hbm), custom_call_target="tpu_custom_call" | custom-call | tf_op jit(solution)/shard_map/exchange/pallas_call | solution.py:499
  73.1 1.6 %store.1 = (f32[3,256,256]{2,1,0:T(8,128)}, f32[256,256]{1,0:T(8,128)}, f32[35,1024]{1,0:T(8,128)}, f32[35,9344]{1,0:T(8,128)}) custom-call(f32[4,256,256]{2,1,0:T(8,128)S(1)} %get-tuple-element.11.landed, f32[35,1024]{1,0:T(8,128)S(1)} %get-tuple-element.12.leaf_moments, f32[35,9344]{1,0:T(8,128)S(1)} %get-tuple-element.13.tree), custom_call_target="tpu_custom_call" | custom-call | tf_op jit(solution)/shard_map/store/pallas_call | solution.py:534
